TPU v7x, 32 devices: a whole 2x2x4 slice. The times are simulated.
32 devices in a mesh: rec: 4 (over z), tm: 8 (over y, x, core).
Axes of the slice: x: 2, y: 2, z: 4, core: 2. Of those that a mesh axis runs over, the one named last changes fastest.
Arguments:
- audio: float32 [4, 40960], P('rec', 'tm'), may hold values from -100 to 100, as said below
- conv0_weight: float32 [10, 512], replicated, may hold values from -2 to 2
- norm_gain: float32 [512], replicated, may hold values from 0.25 to 1.75
- norm_bias: float32 [512], replicated, may hold values from -3 to 3
- conv1_weight: bfloat16 [1536, 512], replicated, may hold values from -0.25 to 0.25
- conv2_weight: bfloat16 [1536, 512], replicated, may hold values from -0.25 to 0.25
- cotangent: bfloat16 [4, 2048, 512], P('rec', 'tm'), may hold values from -0.09375 to 0.09375
Outputs:
- features: bfloat16 [4, 2048, 512], P('rec', 'tm')
- grad_conv0: float32 [10, 512], replicated
- grad_gain: float32 [512], replicated
- grad_bias: float32 [512], replicated
- grad_conv1: float32 [1536, 512], replicated
- grad_conv2: float32 [1536, 512], replicated
Inputs may be any that keep to these rules, and one draw needn't show every extreme that they name: `audio`: recorded waveforms, one row a recording.
All inputs are finite; a program needn't handle non-finite values.
Results may differ from a plain program's by a relative error of at most 0.0095.
Values may be sent and summed in bfloat16 or wider, within the bound.
A program may use at most 64 MiB of HBM per device.

v0:
```python
import jax
import jax.numpy as jnp
from jax import lax
from jax.sharding import PartitionSpec as P

EPS = 1e-05
HIGH = lax.Precision.HIGHEST


def from_behind(value, axis, steps):
    count = lax.axis_size(axis)
    leading, last = (max(0, -steps), min(count, count - steps))
    return lax.ppermute(value, axis, [(source, source + steps) for source in range(leading, last)])


def gelu_slope(value):
    return (
        0.5 * (1.0 + lax.erf(value * 0.7071067811865476))
        + value * jnp.exp(-0.5 * value * value) * 0.3989422804014327
    )


def stride_conv(active, weight):
    records, frames_in, channels = active.shape
    edge_row = from_behind(active[:, :1, :], "tm", -1)
    pairs = active.reshape(records, frames_in // 2, 2 * channels)
    following = jnp.concatenate([pairs[:, 1:, :channels], edge_row], 1)
    output = jnp.einsum(
        "rtk,kc->rtc", pairs, weight[: 2 * channels], preferred_element_type=jnp.float32
    )
    output = output + jnp.einsum(
        "rtk,kc->rtc", following, weight[2 * channels :], preferred_element_type=jnp.float32
    )
    return (pairs, following, output)


def weight_grad(pairs, following, delta):
    upper = jnp.einsum("rtk,rtc->kc", pairs, delta, preferred_element_type=jnp.float32)
    lower = jnp.einsum("rtk,rtc->kc", following, delta, preferred_element_type=jnp.float32)
    return jnp.concatenate([upper, lower], 0)


def stride_back(delta, weight):
    records, frames_out, channels = delta.shape
    edge_row = from_behind(delta[:, -1:, :], "tm", 1)
    before = jnp.concatenate([edge_row, delta[:, :-1, :]], 1)
    back_pairs = jnp.einsum(
        "rtc,kc->rtk", delta, weight[: 2 * channels], preferred_element_type=jnp.float32
    )
    shifted = jnp.einsum(
        "rtc,kc->rtk", before, weight[2 * channels :], preferred_element_type=jnp.float32
    )
    even_rows = back_pairs[:, :, :channels] + shifted
    joined = jnp.concatenate([even_rows, back_pairs[:, :, channels:]], 2)
    return joined.reshape(records, 2 * frames_out, channels)


def shards(audio, conv0_weight, norm_gain, norm_bias, conv1_weight, conv2_weight, cotangent):
    records = audio.shape[0]
    blocks = audio.reshape(records, audio.shape[1] // 5, 5)
    count = float(blocks.shape[1] * lax.axis_size("tm"))
    sample_edge = from_behind(blocks[:, :1, :], "tm", -1)
    following = jnp.concatenate([blocks[:, 1:, :], sample_edge], 1)
    patches = jnp.concatenate([blocks, following], 2)
    pre_norm = jnp.einsum("rtk,kc->rtc", patches, conv0_weight, precision=HIGH)
    first, second = lax.psum((jnp.sum(pre_norm, 1), jnp.sum(pre_norm * pre_norm, 1)), "tm")
    mean = first / count
    variance = second / count - mean * mean
    centered = pre_norm - mean[:, None, :]
    inverse = lax.rsqrt(variance + EPS)
    normed = centered * inverse[:, None, :]
    shifted_norm = normed * norm_gain + norm_bias
    act0 = jax.nn.gelu(shifted_norm, approximate=False).astype(jnp.bfloat16)
    pairs1, follow1, pre1 = stride_conv(act0, conv1_weight)
    act1 = jax.nn.gelu(pre1, approximate=False).astype(jnp.bfloat16)
    pairs2, follow2, pre2 = stride_conv(act1, conv2_weight)
    features = jax.nn.gelu(pre2, approximate=False).astype(jnp.bfloat16)
    delta2 = (cotangent.astype(jnp.float32) * gelu_slope(pre2)).astype(jnp.bfloat16)
    grad_two = weight_grad(pairs2, follow2, delta2)
    back1 = stride_back(delta2, conv2_weight)
    delta1 = (back1 * gelu_slope(pre1)).astype(jnp.bfloat16)
    grad_one = weight_grad(pairs1, follow1, delta1)
    back0 = stride_back(delta1, conv1_weight)
    dnorm = back0 * gelu_slope(shifted_norm)
    local_one = jnp.sum(dnorm, 1)
    local_two = jnp.sum(dnorm * normed, 1)
    sum_one, sum_two = lax.psum((local_one, local_two), "tm")
    scale = norm_gain * inverse
    dpre = scale[:, None, :] * (
        dnorm - (sum_one / count)[:, None, :] - normed * (sum_two / count)[:, None, :]
    )
    grad_zero = jnp.einsum("rtk,rtc->kc", patches, dpre, precision=HIGH)
    norm_terms = jnp.stack([jnp.sum(local_two, 0), jnp.sum(local_one, 0)], 0)
    grad_zero, norm_terms, grad_one, grad_two = lax.psum(
        (grad_zero, norm_terms, grad_one, grad_two), ("rec", "tm")
    )
    return (features, grad_zero, norm_terms[0], norm_terms[1], grad_one, grad_two)


def solution(mesh):
    return jax.shard_map(
        shards,
        mesh=mesh,
        in_specs=(P("rec", "tm"), P(), P(), P(), P(), P(), P("rec", "tm", None)),
        out_specs=(P("rec", "tm", None), P(), P(), P(), P(), P()),
        check_vma=False,
    )
```

profile of v0, /device:TPU:0, one launch (start us, length us, event | category | flops | bytes accessed | tf_op | source)
XLA Modules:
  0.0 249.6 jit_solution(3588708600532290643)
XLA Ops:
  7.7 1.4 reduce.11
  9.6 1.3 collective-permute-start
  11.3 1.3 collective-permute-done
  12.8 1.9 fusion.93
  14.7 15.5 %all-reduce.3 = (f32[1,512]{1,0:T(1,128)S(1)}, f32[1,512]{1,0:T(1,128)S(1)}) all-reduce(f32[1,512]{1,0:T(1,128)S(1)} %bitcast.99, f32[1,512]{1,0:T(1,128)S(1)} %bitcast.98), channel_id=1, replica_groups=mesh['rec'=4,'tm'=8] {'tm'}, use_global_device_ids=true, to_apply=%region_3.0 | all-reduce | flops 1024 | bytes 8192 | tf_op jit(solution)/shard_map/psum | solution.py:66
  30.2 4.9 %fusion.2 = bf16[1024,512]{1,0:T(8,128)(2,1)S(1)} fusion(f32[1024,512]{1,0:T(8,128)S(1)} %get-tuple-element.24, f32[512]{0:T(512)S(1)} %copy-done.8, f32[512]{0:T(512)S(1)} %copy-done.7, f32[512]{0:T(512)S(1)} %bitcast.82, f32[512]{0:T(512)S(1)} %bitcast.86), kind=kLoop, calls=%fused_computation.6 | loop fusion | flops 36175872 | bytes 3153920 | tf_op jit(solution)/shard_map/convert_element_type | solution.py:73
  35.2 5.7 %fusion.106 = bf16[1,1024,512]{2,1,0:T(8,128)(2,1)} fusion(f32[512]{0:T(512)S(1)} %copy-done.8, f32[512]{0:T(512)S(1)} %copy-done.7, f32[512]{0:T(512)S(1)} %bitcast.83, f32[1024,512]{1,0:T(8,128)S(1)} %get-tuple-element.24, f32[512]{0:T(512)S(1)} %bitcast.87), kind=kLoop, calls=%fused_computation.151 | loop fusion | flops 36175872 | bytes 3153920 | tf_op jit(solution)/shard_map/convert_element_type | solution.py:73
  42.7 1.3 collective-permute-start.1
  44.0 3.2 %fusion.47 = f32[512,512]{1,0:T(8,128)} fusion(bf16[512,1024]{1,0:T(8,128)(2,1)} %reshape.357, bf16[1536,512]{1,0:T(8,128)(2,1)} %param.11), kind=kOutput, calls=%fused_computation.81 | convolution fusion | flops 536870912 | bytes 3145728 | tf_op jit(solution)/shard_map/rtk,kc->rtc/dot_general | solution.py:28
  48.3 1.2 slice.86
  49.5 4.9 %fusion.24 = (bf16[512,512]{1,0:T(8,128)(2,1)S(1)}, f32[512,512]{1,0:T(8,128)}) fusion(f32[512,512]{1,0:T(8,128)} %fusion.47, bf16[1536,512]{1,0:T(8,128)(2,1)} %param.11, bf16[1,1,512]{2,1,0:T(2,128)(2,1)S(1)} %collective-permute-done.1, bf16[1,511,512]{2,1,0:T(8,128)(2,1)S(1)} %slice.86), kind=kOutput, calls=%fused_computation.49 | convolution fusion | flops 286785536 | bytes 3670016 | tf_op jit(solution)/shard_map/rtk,kc->rtc/dot_general | solution.py:31
  54.7 1.4 collective-permute-start.2
  56.1 2.5 fusion.44
  60.6 2.5 fusion.58
  63.5 3.8 %collective-permute-start.3 = (bf16[1,1,512]{2,1,0:T(2,128)(2,1)S(1)}, bf16[1,1,512]{2,1,0:T(2,128)(2,1)S(1)}, u32[]{:S(2)}, u32[]{:S(2)}) collective-permute-start(bf16[1,1,512]{2,1,0:T(2,128)(2,1)S(1)} %slice.91), channel_id=1, source_target_pairs={{0,1},{1,2},{2,3},{3,4},{4,5},{5,6},{6,7},{8,9},{9,10},{10,11},{11... | collective-permute-start | bytes 3080 | tf_op jit(solution)/shard_map/ppermute | solution.py:13
  67.7 2.0 pad_maximum_fusion.1
  70.7 1.2 reshape.365
  71.8 2.1 fusion.30
  75.4 2.0 pad_maximum_fusion
  78.4 1.8 fusion.80
  80.3 3.6 %collective-permute-start.4 = (bf16[1,1,512]{2,1,0:T(2,128)(2,1)S(1)}, bf16[1,1,512]{2,1,0:T(2,128)(2,1)S(1)}, u32[]{:S(2)}, u32[]{:S(2)}) collective-permute-start(bf16[1,1,512]{2,1,0:T(2,128)(2,1)S(1)} %slice.95), channel_id=1, source_target_pairs={{0,1},{1,2},{2,3},{3,4},{4,5},{5,6},{6,7},{8,9},{9,10},{10,11},{11... | collective-permute-start | bytes 3080 | tf_op jit(solution)/shard_map/ppermute | solution.py:13
  83.9 2.0 convolution_bitcast_fusion
  86.0 1.6 fusion.20
  87.6 1.5 pad_maximum_fusion.2
  89.0 2.8 %reshape.367 = f32[1024,512]{1,0:T(8,128)} reshape(f32[1,512,1024]{2,1,0:T(8,128)} %pad_maximum_fusion.2) | data formatting | bytes 4194304 | tf_op jit(solution)/shard_map/reshape | solution.py:55
  91.8 3.6 %fusion.92 = (f32[512]{0:T(512)S(1)}, f32[512]{0:T(512)S(1)}, f32[1024,512]{1,0:T(8,128)}) fusion(f32[512]{0:T(512)S(1)} %bitcast.84, f32[1024,512]{1,0:T(8,128)S(1)} %get-tuple-element.24, f32[512]{0:T(512)S(1)} %bitcast.88, f32[1024,512]{1,0:T(8,128)} %reshape.367, f32[512]{0:T(512)S(1)} %copy-done.8, f32[512]{0:T(512)S(1)} %copy-done.7), kind=kLoop, calls=%fused_computation.146 | loop fusion | flops 8387584 | bytes 6303744 | tf_op jit(solution)/shard_map/reduce_sum | solution.py:85
  95.4 12.9 %all-reduce.2 = (f32[1,512]{1,0:T(1,128)S(1)}, f32[1,512]{1,0:T(1,128)S(1)}) all-reduce(f32[1,512]{1,0:T(1,128)S(1)} %bitcast.93, f32[1,512]{1,0:T(1,128)S(1)} %bitcast.91), channel_id=1, replica_groups=mesh['rec'=4,'tm'=8] {'tm'}, use_global_device_ids=true, to_apply=%region_7.0 | all-reduce | flops 1024 | bytes 8192 | tf_op jit(solution)/shard_map/psum | solution.py:87
  108.3 3.1 %fusion.8 = f32[10,512]{1,0:T(8,128)S(1)} fusion(f32[1024,512]{1,0:T(8,128)} %get-tuple-element.20, f32[1024,512]{1,0:T(8,128)S(1)} %get-tuple-element.24, f32[512]{0:T(512)S(1)} %bitcast.96, f32[512]{0:T(512)S(1)} %bitcast.97, f32[512]{0:T(512)S(1)} %bitcast.95, f32[512]{0:T(512)S(1)} %bitcast.85, f32[512]{0:T(512)S(1)} %bitcast.89, ...), kind=kOutput, calls=%fused_computation.13 | convolution fusion | flops 66060288 | bytes 4265984 | tf_op jit(solution)/shard_map/rtk,rtc->kc/dot_general | solution.py:92
  111.5 42.1 %all-reduce = (f32[10,512]{1,0:T(8,128)}, f32[2,512]{1,0:T(2,128)S(1)}) all-reduce(f32[10,512]{1,0:T(8,128)S(1)} %fusion.8, f32[2,512]{1,0:T(2,128)S(1)} %pad_maximum_fusion.4), channel_id=1, replica_groups=mesh['rec'=4,'tm'=8] {'rec','tm'}, use_global_device_ids=true, to_apply=%region_8.0 | all-reduce | flops 6144 | bytes 49152 | tf_op jit(solution)/shard_map/psum | solution.py:94
  154.2 82.8 %all-reduce.6.cloned.1.call-done = (f32[1536,512]{1,0:T(8,128)}, f32[1536,512]{1,0:T(8,128)}) async-done(((f32[1536,512]{1,0:T(8,128)}, f32[1536,512]{1,0:T(8,128)}), (f32[1536,512]{1,0:T(8,128)}, f32[1536,512]{1,0:T(8,128)})) %all-reduce.6.cloned.1.call-update) | async-done | bytes 6291472 | tf_op jit(solution)/shard_map/psum | solution.py:94
  237.0 4.0 %copy.33 = f32[1536,512]{1,0:T(8,128)} copy(f32[1536,512]{1,0:T(8,128)} %get-tuple-element.35) | data formatting | bytes 6291456
  241.1 1.7 copy.34
  (56 shorter events, 11.7 us)
Async XLA Ops:
  7.2 5.6 %copy-start = (f32[10,512]{1,0:T(8,128)S(1)}, f32[10,512]{1,0:T(8,128)}, u32[]{:S(2)}) copy-start(f32[10,512]{1,0:T(8,128)} %param.8) | copy-start | bytes 61444
  7.2 229.8 %all-reduce.6.cloned.1.call-start = ((), (), s32[]{:S(2)}) async-start(), calls=%async_computation | async-start | bytes 12582912 | tf_op jit(solution)/shard_map/psum | solution.py:94
  9.5 20.7 %copy-start.7 = (f32[512]{0:T(512)S(1)}, f32[512]{0:T(512)}, u32[]{:S(2)}) copy-start(f32[512]{0:T(512)} %param.9) | copy-start | bytes 6148
  9.5 20.7 %copy-start.8 = (f32[512]{0:T(512)S(1)}, f32[512]{0:T(512)}, u32[]{:S(2)}) copy-start(f32[512]{0:T(512)} %param.10) | copy-start | bytes 6148
  9.6 3.0 %collective-permute-start = (f32[1,1,5]{2,1,0:T(1,128)S(1)}, f32[1,1,5]{2,1,0:T(1,128)S(1)}, u32[]{:S(2)}, u32[]{:S(2)}) collective-permute-start(f32[1,1,5]{2,1,0:T(1,128)S(1)} %slice.85), channel_id=1, source_target_pairs={{1,0},{2,1},{3,2},{4,3},{5,4},{6,5},{7,6},{9,8},{10,9},{11,10},{12... | collective-permute-start | bytes 68 | tf_op jit(solution)/shard_map/ppermute | solution.py:13
  42.7 6.8 %collective-permute-start.1 = (bf16[1,1,512]{2,1,0:T(2,128)(2,1)S(1)}, bf16[1,1,512]{2,1,0:T(2,128)(2,1)S(1)}, u32[]{:S(2)}, u32[]{:S(2)}) collective-permute-start(bf16[1,1,512]{2,1,0:T(2,128)(2,1)S(1)} %slice.87), channel_id=1, source_target_pairs={{1,0},{2,1},{3,2},{4,3},{5,4},{6,5},{7,6},{9,8},{10,9},{11,10},{12... | collective-permute-start | bytes 3080 | tf_op jit(solution)/shard_map/ppermute | solution.py:13
  49.5 5.0 %copy-start.5 = (bf16[1,511,512]{2,1,0:T(8,128)(2,1)}, bf16[1,511,512]{2,1,0:T(8,128)(2,1)S(1)}, u32[]{:S(2)}) copy-start(bf16[1,511,512]{2,1,0:T(8,128)(2,1)S(1)} %slice.86) | copy-start | bytes 1569796
  54.6 5.9 %copy-start.9 = (bf16[1,256,512]{2,1,0:T(8,128)(2,1)S(1)}, bf16[1,256,512]{2,1,0:T(8,128)(2,1)}, u32[]{:S(2)}) copy-start(bf16[1,256,512]{2,1,0:T(8,128)(2,1)} %param.13) | copy-start | bytes 786436
  54.7 5.9 %collective-permute-start.2 = (bf16[1,1,512]{2,1,0:T(2,128)(2,1)S(1)}, bf16[1,1,512]{2,1,0:T(2,128)(2,1)S(1)}, u32[]{:S(2)}, u32[]{:S(2)}) collective-permute-start(bf16[1,1,512]{2,1,0:T(2,128)(2,1)S(1)} %slice.89), channel_id=1, source_target_pairs={{1,0},{2,1},{3,2},{4,3},{5,4},{6,5},{7,6},{9,8},{10,9},{11,10},{12... | collective-permute-start | bytes 3080 | tf_op jit(solution)/shard_map/ppermute | solution.py:13
  63.5 6.7 %collective-permute-start.3 = (bf16[1,1,512]{2,1,0:T(2,128)(2,1)S(1)}, bf16[1,1,512]{2,1,0:T(2,128)(2,1)S(1)}, u32[]{:S(2)}, u32[]{:S(2)}) collective-permute-start(bf16[1,1,512]{2,1,0:T(2,128)(2,1)S(1)} %slice.91), channel_id=1, source_target_pairs={{0,1},{1,2},{2,3},{3,4},{4,5},{5,6},{6,7},{8,9},{9,10},{10,11},{11... | collective-permute-start | bytes 3080 | tf_op jit(solution)/shard_map/ppermute | solution.py:13
  67.7 2.0 copy-start.3
  71.8 2.1 copy-start.1
  73.9 1.0 copy-start.6
  77.4 1.0 copy-start.4
  80.3 5.7 %collective-permute-start.4 = (bf16[1,1,512]{2,1,0:T(2,128)(2,1)S(1)}, bf16[1,1,512]{2,1,0:T(2,128)(2,1)S(1)}, u32[]{:S(2)}, u32[]{:S(2)}) collective-permute-start(bf16[1,1,512]{2,1,0:T(2,128)(2,1)S(1)} %slice.95), channel_id=1, source_target_pairs={{0,1},{1,2},{2,3},{3,4},{4,5},{5,6},{6,7},{8,9},{9,10},{10,11},{11... | collective-permute-start | bytes 3080 | tf_op jit(solution)/shard_map/ppermute | solution.py:13
  237.0 4.0 %copy-start.2 = (f32[1536,512]{1,0:T(8,128)S(1)}, f32[1536,512]{1,0:T(8,128)}, u32[]{:S(2)}) copy-start(f32[1536,512]{1,0:T(8,128)} %get-tuple-element.36) | copy-start | bytes 9437188
Sparse Core Ops, SparseCore 0:
  77.5 159.4 all-reduce.5
where the time goes:
time: 251 us; the launch traced here: 250 us
  waiting for transfers between devices  84.2 us (34%)
  blocking collectives  70.5 us (28%)
  other arithmetic  25.2 us (10%)
  matrix products  24.5 us (10%)
  local copies, waits for them, and re-layouts  19.4 us (8%)
  between operations  14.3 us (6%)
  starting transfers between devices  11.5 us (5%)
    psum x1, waiting for transfers between devices, shards(): lax.psum((grad_zero, norm_terms, grad_one, grad_two), ('rec', 'tm'))  82.8 us
    psum x1, blocking collectives, shards(): lax.psum((grad_zero, norm_terms, grad_one, grad_two), ('rec', 'tm'))  42.1 us
    psum x1, blocking collectives, shards(): lax.psum((jnp.sum(pre_norm, 1), jnp.sum(pre_norm * pre_norm, 1)), 'tm')  15.5 us
    psum x1, blocking collectives, shards(): sum_one, sum_two = lax.psum((local_one, local_two), 'tm')  12.9 us
    ppermute x5, starting transfers between devices, from_behind(): lax.ppermute(value, axis, [(source, source + steps) for source in range(l...  11.5 us
    convert_element_type x2, other arithmetic, shards(): act0 = jax.nn.gelu(shifted_norm, approximate=False).astype(jnp.bfloat16)  10.6 us
    unnamed x23, local copies, waits for them, and re-layouts  7.54 us
    dot_general x2, matrix products, stride_conv(): jnp.einsum('rtk,kc->rtc', following, weight[2 * channels:], preferred_ele...  7.41 us
  transfers between devices with their start and end apart: 6, of which 2 were waited for; matrix products, arithmetic and copies ran while one was open for 12% of the time, Pallas kernels for 0%

commit v1 on v0

--- a/solution.py
+++ b/solution.py
@@ -5,6 +5,11 @@
 
 EPS = 1e-05
 HIGH = lax.Precision.HIGHEST
+
+
+def axis_by_axis(array, one, other):
+    partial = lax.psum(array, one)
+    return lax.psum(partial, other)
 
 
 def from_behind(value, axis, steps):
@@ -91,8 +96,8 @@
     )
     grad_zero = jnp.einsum("rtk,rtc->kc", patches, dpre, precision=HIGH)
     norm_terms = jnp.stack([jnp.sum(local_two, 0), jnp.sum(local_one, 0)], 0)
-    grad_zero, norm_terms, grad_one, grad_two = lax.psum(
-        (grad_zero, norm_terms, grad_one, grad_two), ("rec", "tm")
+    grad_zero, norm_terms, grad_one, grad_two = axis_by_axis(
+        (grad_zero, norm_terms, grad_one, grad_two), "tm", "rec"
     )
     return (features, grad_zero, norm_terms[0], norm_terms[1], grad_one, grad_two)
 

time: 251 us -> 426 us (1.70)
  waiting for transfers between devices: 84.2 us -> 251 us
  blocking collectives: 70.5 us -> 81.4 us
    psum x1 -> x2, waiting for transfers between devices: 82.8 us -> 250 us  [the longest x1 142 us: axis_by_axis(): return lax.psum(partial, other)]
    psum x1 -> x2, blocking collectives: 42.1 us -> 51.3 us  [the longest x1 27 us: axis_by_axis(): return lax.psum(partial, other)]
  transfers between devices with their start and end apart: 6 -> 7, of which waited for: 2 -> 3; matrix products, arithmetic and copies ran while one was open for 12% -> 7% of each run, Pallas kernels for 0% -> 0%
where the time goes in v1:
time: 426 us; the launch traced here: 425 us
  waiting for transfers between devices  251 us (59%)
  blocking collectives  81.4 us (19%)
  other arithmetic  25 us (6%)
  matrix products  24.5 us (6%)
  local copies, waits for them, and re-layouts  19.4 us (5%)
  between operations  14.3 us (3%)
  starting transfers between devices  9.55 us (2%)
    psum x1, waiting for transfers between devices, axis_by_axis(): return lax.psum(partial, other)  142 us
    psum x1, waiting for transfers between devices, axis_by_axis(): partial = lax.psum(array, one)  108 us
    psum x1, blocking collectives, axis_by_axis(): return lax.psum(partial, other)  27 us
    psum x1, blocking collectives, axis_by_axis(): partial = lax.psum(array, one)  24.3 us
    psum x1, blocking collectives, shards(): lax.psum((jnp.sum(pre_norm, 1), jnp.sum(pre_norm * pre_norm, 1)), 'tm')  15.5 us
    psum x1, blocking collectives, shards(): sum_one, sum_two = lax.psum((local_one, local_two), 'tm')  14.6 us
    convert_element_type x2, other arithmetic, shards(): act0 = jax.nn.gelu(shifted_norm, approximate=False).astype(jnp.bfloat16)  10.6 us
    ppermute x5, starting transfers between devices, from_behind(): lax.ppermute(value, axis, [(source, source + steps) for source in range(l...  9.47 us
  transfers between devices with their start and end apart: 7, of which 3 were waited for; matrix products, arithmetic and copies ran while one was open for 7% of the time, Pallas kernels for 0%

profile of v1, /device:TPU:0, one launch (start us, length us, event | category | flops | bytes accessed | tf_op | source)
XLA Modules:
  0.0 425.0 jit_solution(10214376043737384646)
XLA Ops:
  7.7 1.4 reduce.11
  9.6 1.3 collective-permute-start
  11.3 1.3 collective-permute-done
  12.8 1.9 fusion.93
  14.7 15.5 %all-reduce.2 = (f32[1,512]{1,0:T(1,128)S(1)}, f32[1,512]{1,0:T(1,128)S(1)}) all-reduce(f32[1,512]{1,0:T(1,128)S(1)} %bitcast.99, f32[1,512]{1,0:T(1,128)S(1)} %bitcast.98), channel_id=1, replica_groups=mesh['rec'=4,'tm'=8] {'tm'}, use_global_device_ids=true, to_apply=%region_3.0 | all-reduce | flops 1024 | bytes 8192 | tf_op jit(solution)/shard_map/psum | solution.py:71
  30.2 4.9 %fusion.2 = bf16[1024,512]{1,0:T(8,128)(2,1)S(1)} fusion(f32[1024,512]{1,0:T(8,128)S(1)} %get-tuple-element.28, f32[512]{0:T(512)S(1)} %copy-done.8, f32[512]{0:T(512)S(1)} %copy-done.7, f32[512]{0:T(512)S(1)} %bitcast.82, f32[512]{0:T(512)S(1)} %bitcast.86), kind=kLoop, calls=%fused_computation.6 | loop fusion | flops 36175872 | bytes 3153920 | tf_op jit(solution)/shard_map/convert_element_type | solution.py:78
  35.2 5.7 %fusion.106 = bf16[1,1024,512]{2,1,0:T(8,128)(2,1)} fusion(f32[512]{0:T(512)S(1)} %copy-done.8, f32[512]{0:T(512)S(1)} %copy-done.7, f32[512]{0:T(512)S(1)} %bitcast.83, f32[1024,512]{1,0:T(8,128)S(1)} %get-tuple-element.28, f32[512]{0:T(512)S(1)} %bitcast.87), kind=kLoop, calls=%fused_computation.151 | loop fusion | flops 36175872 | bytes 3153920 | tf_op jit(solution)/shard_map/convert_element_type | solution.py:78
  42.7 1.3 collective-permute-start.1
  44.0 3.2 fusion.47
  49.5 4.9 %fusion.24 = (bf16[512,512]{1,0:T(8,128)(2,1)S(1)}, f32[512,512]{1,0:T(8,128)}) fusion(f32[512,512]{1,0:T(8,128)} %fusion.47, bf16[1536,512]{1,0:T(8,128)(2,1)} %param.11, bf16[1,1,512]{2,1,0:T(2,128)(2,1)S(1)} %collective-permute-done.1, bf16[1,511,512]{2,1,0:T(8,128)(2,1)S(1)} %slice.86), kind=kOutput, calls=%fused_computation.49 | convolution fusion | flops 286785536 | bytes 3670016 | tf_op jit(solution)/shard_map/rtk,kc->rtc/dot_general | solution.py:36
  54.7 1.4 collective-permute-start.2
  56.1 2.5 fusion.44
  60.6 2.5 fusion.58
  63.5 3.8 collective-permute-start.3
  67.7 2.0 pad_maximum_fusion.1
  71.9 2.1 fusion.30
  75.4 2.0 pad_maximum_fusion
  77.5 107.6 %all-reduce.9.cloned.1.call-done = (f32[1536,512]{1,0:T(8,128)}, f32[1536,512]{1,0:T(8,128)}) async-done(((f32[1536,512]{1,0:T(8,128)}, f32[1536,512]{1,0:T(8,128)}), (f32[1536,512]{1,0:T(8,128)}, f32[1536,512]{1,0:T(8,128)})) %all-reduce.9.cloned.1.call-update) | async-done | bytes 6291472 | tf_op jit(solution)/shard_map/psum | solution.py:11
  186.1 1.8 fusion.80
  187.9 1.6 collective-permute-start.4
  189.6 2.0 convolution_bitcast_fusion
  191.6 1.5 fusion.20
  193.2 1.5 pad_maximum_fusion.2
  194.6 2.7 reshape.367
  197.4 3.5 fusion.92
  200.9 14.6 %all-reduce.1 = (f32[1,512]{1,0:T(1,128)S(1)}, f32[1,512]{1,0:T(1,128)S(1)}) all-reduce(f32[1,512]{1,0:T(1,128)S(1)} %bitcast.93, f32[1,512]{1,0:T(1,128)S(1)} %bitcast.91), channel_id=1, replica_groups=mesh['rec'=4,'tm'=8] {'tm'}, use_global_device_ids=true, to_apply=%region_7.0 | all-reduce | flops 1024 | bytes 8192 | tf_op jit(solution)/shard_map/psum | solution.py:92
  215.5 3.1 fusion.8
  218.6 24.3 %all-reduce = (f32[10,512]{1,0:T(8,128)S(1)}, f32[2,512]{1,0:T(2,128)S(1)}) all-reduce(f32[10,512]{1,0:T(8,128)S(1)} %fusion.8, f32[2,512]{1,0:T(2,128)S(1)} %pad_maximum_fusion.4), channel_id=1, replica_groups=mesh['rec'=4,'tm'=8] {'tm'}, use_global_device_ids=true, to_apply=%region_8.0 | all-reduce | flops 6144 | bytes 49152 | tf_op jit(solution)/shard_map/psum | solution.py:11
  242.9 27.0 %all-reduce.4 = (f32[10,512]{1,0:T(8,128)}, f32[2,512]{1,0:T(2,128)S(1)}) all-reduce(f32[10,512]{1,0:T(8,128)S(1)} %get-tuple-element.10, f32[2,512]{1,0:T(2,128)S(1)} %get-tuple-element.11), channel_id=1, replica_groups=mesh['rec'=4,'tm'=8] {'rec'}, use_global_device_ids=true, to_apply=%region_9.0 | all-reduce | flops 6144 | bytes 49152 | tf_op jit(solution)/shard_map/psum | solution.py:12
  270.5 142.0 %all-reduce.11.cloned.1.call-done = (f32[1536,512]{1,0:T(8,128)}, f32[1536,512]{1,0:T(8,128)}) async-done(((f32[1536,512]{1,0:T(8,128)}, f32[1536,512]{1,0:T(8,128)}), (f32[1536,512]{1,0:T(8,128)}, f32[1536,512]{1,0:T(8,128)})) %all-reduce.11.cloned.1.call-update) | async-done | bytes 6291472 | tf_op jit(solution)/shard_map/psum | solution.py:12
  412.5 4.0 copy.35
  416.5 1.7 copy.36
  (60 shorter events, 14.1 us)
Async XLA Ops:
  7.2 5.6 %copy-start = (f32[10,512]{1,0:T(8,128)S(1)}, f32[10,512]{1,0:T(8,128)}, u32[]{:S(2)}) copy-start(f32[10,512]{1,0:T(8,128)} %param.8) | copy-start | bytes 61444
  7.2 177.9 %all-reduce.9.cloned.1.call-start = ((), (), s32[]{:S(2)}) async-start(), calls=%async_computation | async-start | bytes 12582912 | tf_op jit(solution)/shard_map/psum | solution.py:11
  9.5 20.7 %copy-start.7 = (f32[512]{0:T(512)S(1)}, f32[512]{0:T(512)}, u32[]{:S(2)}) copy-start(f32[512]{0:T(512)} %param.9) | copy-start | bytes 6148
  9.5 20.7 %copy-start.8 = (f32[512]{0:T(512)S(1)}, f32[512]{0:T(512)}, u32[]{:S(2)}) copy-start(f32[512]{0:T(512)} %param.10) | copy-start | bytes 6148
  9.6 3.0 collective-permute-start
  42.7 6.8 %collective-permute-start.1 = (bf16[1,1,512]{2,1,0:T(2,128)(2,1)S(1)}, bf16[1,1,512]{2,1,0:T(2,128)(2,1)S(1)}, u32[]{:S(2)}, u32[]{:S(2)}) collective-permute-start(bf16[1,1,512]{2,1,0:T(2,128)(2,1)S(1)} %slice.87), channel_id=1, source_target_pairs={{1,0},{2,1},{3,2},{4,3},{5,4},{6,5},{7,6},{9,8},{10,9},{11,10},{12... | collective-permute-start | bytes 3080 | tf_op jit(solution)/shard_map/ppermute | solution.py:18
  49.5 5.0 %copy-start.5 = (bf16[1,511,512]{2,1,0:T(8,128)(2,1)}, bf16[1,511,512]{2,1,0:T(8,128)(2,1)S(1)}, u32[]{:S(2)}) copy-start(bf16[1,511,512]{2,1,0:T(8,128)(2,1)S(1)} %slice.86) | copy-start | bytes 1569796
  54.6 5.9 %copy-start.9 = (bf16[1,256,512]{2,1,0:T(8,128)(2,1)S(1)}, bf16[1,256,512]{2,1,0:T(8,128)(2,1)}, u32[]{:S(2)}) copy-start(bf16[1,256,512]{2,1,0:T(8,128)(2,1)} %param.13) | copy-start | bytes 786436
  54.7 5.9 %collective-permute-start.2 = (bf16[1,1,512]{2,1,0:T(2,128)(2,1)S(1)}, bf16[1,1,512]{2,1,0:T(2,128)(2,1)S(1)}, u32[]{:S(2)}, u32[]{:S(2)}) collective-permute-start(bf16[1,1,512]{2,1,0:T(2,128)(2,1)S(1)} %slice.89), channel_id=1, source_target_pairs={{1,0},{2,1},{3,2},{4,3},{5,4},{6,5},{7,6},{9,8},{10,9},{11,10},{12... | collective-permute-start | bytes 3080 | tf_op jit(solution)/shard_map/ppermute | solution.py:18
  63.5 6.7 %collective-permute-start.3 = (bf16[1,1,512]{2,1,0:T(2,128)(2,1)S(1)}, bf16[1,1,512]{2,1,0:T(2,128)(2,1)S(1)}, u32[]{:S(2)}, u32[]{:S(2)}) collective-permute-start(bf16[1,1,512]{2,1,0:T(2,128)(2,1)S(1)} %slice.91), channel_id=1, source_target_pairs={{0,1},{1,2},{2,3},{3,4},{4,5},{5,6},{6,7},{8,9},{9,10},{10,11},{11... | collective-permute-start | bytes 3080 | tf_op jit(solution)/shard_map/ppermute | solution.py:18
  67.7 2.0 copy-start.3
  71.9 2.1 copy-start.1
  73.9 1.0 copy-start.6
  77.4 335.1 %all-reduce.11.cloned.1.call-start = ((), (), s32[]{:S(2)}) async-start(), calls=%async_computation.1 | async-start | bytes 12582912 | tf_op jit(solution)/shard_map/psum | solution.py:12
  185.0 1.0 copy-start.4
  187.9 3.7 collective-permute-start.4
  412.5 4.0 copy-start.2
Sparse Core Ops, SparseCore 0:
  77.6 107.4 all-reduce.8
  187.6 224.8 all-reduce.10
